TPU v7x, 256 devices: a whole 4x4x8 slice. The times are simulated.
256 devices in a mesh: section: 8 (over y, x_hi), rep: 32 (over z, x_lo, core).
Axes of the slice: x: 4 (x_hi: 2, x_lo: 2; x = x_hi * 2 + x_lo), y: 4, z: 8, core: 2. Of those that a mesh axis runs over, the one named last changes fastest.
Arguments:
- history: bfloat16 [8, 64, 64, 9216], P('section', 'rep'), may hold values from -6 to 6
- codes: int32 [8, 64, 64, 9216], P('section', 'rep'), may hold values from -128 to 127
- scales: float32 [8, 64, 64], P('section', 'rep'), may hold values from 0.003 to 0.03
- sample_ids: int32 [32, 2], P('rep'), may hold values from 0 to 1, each once within a row
- cotangent: bfloat16 [64, 64, 9216], P('rep'), may hold values from -6 to 6
- ln_gain: float32 [8, 9216], P('section'), may hold values from 0.5 to 1.5
- ln_bias: float32 [8, 9216], P('section'), may hold values from -3 to 3
- down_weight: bfloat16 [8, 9216, 256], P('section', 'rep'), may hold values from -0.1875 to 0.1875
- up_weight: bfloat16 [8, 9216, 256], P('section', 'rep'), may hold values from -0.0625 to 0.0625
Outputs:
- input_grads: bfloat16 [8, 64, 64, 9216], P('section', 'rep')
- adapter_grads: float32 [8, 9216, 512], P('section', 'rep')
Inputs may be any that keep to these rules, and one draw needn't show every extreme that they name: `sample_ids`: each replica's row names every history entry of that replica once.
All inputs are finite; a program needn't handle non-finite values.
Results may differ from a plain program's by a relative error of at most 0.038.
Values may be sent and summed in bfloat16 or wider, within the bound.
A program may use at most 128 MiB of HBM per device.

v0:
```python
import jax
import jax.numpy as jnp
from jax import lax
from jax.sharding import PartitionSpec as P

EPSILON = 1e-05
HALF_ROOT = 0.7071067811865476
DENSITY = 0.3989422804014327


def from_behind(value, axis, steps):
    count = lax.axis_size(axis)
    leading, last = (max(0, -steps), min(count, count - steps))
    return lax.ppermute(value, axis, [(source, source + steps) for source in range(leading, last)])


def unpack_codes(levels):
    return levels.astype(jnp.float32)


def gelu_pair(preact):
    normal_cdf = 0.5 * (1.0 + lax.erf(preact * HALF_ROOT))
    bump = DENSITY * jnp.exp(-0.5 * preact * preact)
    return (preact * normal_cdf, normal_cdf + preact * bump)


def section_inputs(stored, packed, scaling, picks):
    chosen = jnp.take(stored, picks, axis=0).astype(jnp.float32)
    rebuilt = chosen + scaling[..., None] * unpack_codes(packed)
    return rebuilt.astype(jnp.bfloat16).reshape(-1, stored.shape[-1])


def normalize(inputs, gain_row, bias_row):
    values = inputs.astype(jnp.float32)
    centred = values - jnp.mean(values, axis=-1, keepdims=True)
    inv_std = lax.rsqrt(jnp.mean(centred * centred, axis=-1, keepdims=True) + EPSILON)
    scaled = centred * inv_std
    normed = (scaled * gain_row + bias_row).astype(jnp.bfloat16)
    return (normed, scaled, inv_std)


def input_grad(out_grad, back, gain_row, scaled, inv_std):
    weighted = back * gain_row
    inner = (
        weighted
        - jnp.mean(weighted, axis=-1, keepdims=True)
        - scaled * jnp.mean(weighted * scaled, axis=-1, keepdims=True)
    )
    return (out_grad.astype(jnp.float32) + inv_std * inner).astype(jnp.bfloat16)


def contract_rows(left, right):
    return lax.dot_general(
        left, right, (((0,), (0,)), ((), ())), preferred_element_type=jnp.float32
    )


def contract_cols(left, right):
    return lax.dot_general(
        left, right, (((1,), (1,)), ((), ())), preferred_element_type=jnp.float32
    )


def take_rows(source, begin, count):
    return lax.dynamic_slice_in_dim(source, begin, count, 0)


def put_rows(target, active, values, begin):
    older = lax.dynamic_slice_in_dim(target, begin, values.shape[0], 0)
    return lax.dynamic_update_slice_in_dim(target, jnp.where(active, values, older), begin, 0)


def per_device(
    history, codes, scales, sample_ids, cotangent, ln_gain, ln_bias, down_weight, up_weight
):
    sections = lax.axis_size("section")
    position = lax.axis_index("section")
    w_down, w_up = (
        lax.all_gather(down_weight[0], "rep", axis=0, tiled=True),
        lax.all_gather(up_weight[0], "rep", axis=0, tiled=True),
    )
    inputs = section_inputs(history[0], codes[0], scales[0], sample_ids[0])
    gain_row = ln_gain[0]
    bias_row = ln_bias[0]
    normed, scaled, inv_std = normalize(inputs, gain_row, bias_row)
    activated, slopes = gelu_pair(jnp.dot(normed, w_down, preferred_element_type=jnp.float32))
    hidden = activated.astype(jnp.bfloat16)
    tok_count = cotangent.shape[1]
    row_total = inputs.shape[0]
    model_width = inputs.shape[1]
    rank_pair = 2 * w_down.shape[1]
    seeded = cotangent.reshape(row_total, model_width)
    pieces = 1
    block_size = tok_count // pieces
    blocks = row_total // block_size
    tick_count = blocks + sections - 1

    def advance(tick, carry):
        incoming, produced, running, kept_grad, kept_top = carry
        offset = tick - (sections - 1 - position)
        active = jnp.logical_and(offset >= 0, offset < blocks)
        begin = jnp.clip(offset, 0, blocks - 1) * block_size
        top_grad = take_rows(seeded, begin, block_size)
        out_grad = jnp.where(position == sections - 1, top_grad, incoming)
        slope_rows = take_rows(slopes, begin, block_size)
        scaled_rows = take_rows(scaled, begin, block_size)
        inv_rows = take_rows(inv_std, begin, block_size)
        act_grad = (
            jnp.dot(out_grad, w_up, preferred_element_type=jnp.float32) * slope_rows
        ).astype(jnp.bfloat16)
        back = contract_cols(act_grad, w_down)
        result = input_grad(out_grad, back, gain_row, scaled_rows, inv_rows)
        produced = put_rows(produced, active, result, begin)
        normed_rows = take_rows(normed, begin, block_size)
        hidden_rows = take_rows(hidden, begin, block_size)
        terms = jnp.concatenate(
            [contract_rows(normed_rows, act_grad), contract_rows(out_grad, hidden_rows)], axis=1
        )
        running = running + jnp.where(active, terms, 0.0)
        incoming = from_behind(result, "section", -1)
        return (incoming, produced, running, kept_grad, kept_top)

    start_in = jnp.zeros((block_size, model_width), jnp.bfloat16)
    start_out = jnp.zeros((row_total, model_width), jnp.bfloat16)
    start_sum = jnp.zeros((model_width, rank_pair), jnp.float32)
    start_grad = jnp.zeros((1, 1), jnp.bfloat16)
    start_top = jnp.zeros((1, 1), jnp.bfloat16)
    carry = lax.fori_loop(
        0, tick_count, advance, (start_in, start_out, start_sum, start_grad, start_top)
    )
    produced = carry[1]
    summed = lax.psum_scatter(
        (carry[2] / float(tok_count)).astype(jnp.bfloat16), "rep", scatter_dimension=0, tiled=True
    ).astype(jnp.float32)
    return (produced.reshape(1, row_total // tok_count, tok_count, model_width), summed[None])


def solution(mesh):
    return jax.shard_map(
        per_device,
        mesh=mesh,
        in_specs=(
            P("section", "rep", None, None),
            P("section", "rep", None, None),
            P("section", "rep", None),
            P("rep", None),
            P("rep", None, None),
            P("section", None),
            P("section", None),
            P("section", "rep", None),
            P("section", "rep", None),
        ),
        out_specs=(P("section", "rep", None, None), P("section", "rep", None)),
        check_vma=False,
    )
```

profile of v0, /device:TPU:1, one launch (start us, length us, event | category | flops | bytes accessed | tf_op | source)
XLA Modules:
  0.0 694.0 jit_solution(3163378220017021504)
XLA Ops:
  12.3 4.5 convert_reduce_fusion
  18.0 7.1 %add_convert_fusion.1 = (bf16[128,9216]{1,0:T(8,128)(2,1)S(1)}, f32[128,9216]{1,0:T(8,128)}) fusion(f32[9216]{0:T(1024)S(1)} %bitcast.75, f32[9216]{0:T(1024)S(1)} %bitcast.73, f32[128]{0:T(128)S(1)} %rsqrt.20, f32[128]{0:T(128)S(1)} %div.26, s32[1,2,64,9216]{3,2,1,0:T(8,128)} %param.12, f32[128]{0:T(128)S(1)} %mul.192, bf16[2,64,9216]{2,1,0:T(8,128)(2,1)} %gather_fusion, ...), kind=kLoop, calls=%fused_computation.31 | loop fusion | flops 14155776 | bytes 14231168 | tf_op jit(solution)/shard_map/convert_element_type | solution.py:38
  25.1 57.0 %all-gather.7.cloned.1.call-done = bf16[1,9216,256]{2,1,0:T(8,128)(2,1)} async-done(((bf16[1,288,256]{2,1,0:T(8,128)(2,1)}), bf16[1,9216,256]{2,1,0:T(8,128)(2,1)}) %all-gather.7.cloned.1.call-update) | async-done | bytes 4718608 | tf_op jit(solution)/shard_map/all_gather | solution.py:79
  85.9 65.5 %all-gather.5.cloned.1.call-done = bf16[1,9216,256]{2,1,0:T(8,128)(2,1)} async-done(((bf16[1,288,256]{2,1,0:T(8,128)(2,1)}), bf16[1,9216,256]{2,1,0:T(8,128)(2,1)}) %all-gather.5.cloned.1.call-update) | async-done | bytes 4718608 | tf_op jit(solution)/shard_map/all_gather | solution.py:80
  153.2 362.6 %while.20 = (s32[]{:T(128)}, bf16[64,9216]{1,0:T(8,128)(2,1)S(1)}, bf16[128,9216]{1,0:T(8,128)(2,1)}, f32[9216,512]{0,1:T(8,128)}, pred[]{:T(512)}, /*index=5*/s...) while((s32[]{:T(128)}, bf16[64,9216]{1,0:T(8,128)(2,1)S(1)}, ...), condition=%wide.region_5.6_spmd.clone, body=%wide.region_2.0_spmd.clone.sunk | while | flops 1234534400 | bytes 187031632 | solution.py:128
  170.9 8.1 %fusion.58 = f32[9216,512]{0,1:T(8,128)} fusion(f32[9216,256]{0,1:T(8,128)S(1)} %fusion.56, f32[9216,256]{0,1:T(8,128)S(1)} %fusion.57, f32[9216,512]{0,1:T(8,128)} %get-tuple-element.546, pred[]{:T(512)S(6)} %compare.3, pred[]{:T(512)S(6)} %and.21), kind=kLoop, calls=%fused_computation.2.clone.1 | loop fusion | flops 18874368 | bytes 56623104 | tf_op jit(solution)/shard_map/while/body/eval_jaxpr/add | solution.py:119
  179.1 17.3 %collective-permute-done = bf16[64,9216]{1,0:T(8,128)(2,1)S(1)} collective-permute-done((bf16[64,9216]{1,0:T(8,128)(2,1)}, bf16[64,9216]{1,0:T(8,128)(2,1)S(1)}, u32[]{:S(2)}, u32[]{:S(2)}) %collective-permute-start) | collective-permute-done | bytes 1179680 | tf_op jit(solution)/shard_map/while/body/eval_jaxpr/ppermute | solution.py:14
  214.1 15.6 %fusion.58 = f32[9216,512]{0,1:T(8,128)} fusion(f32[9216,256]{0,1:T(8,128)S(1)} %fusion.56, f32[9216,256]{0,1:T(8,128)S(1)} %fusion.57, f32[9216,512]{0,1:T(8,128)} %get-tuple-element.546, pred[]{:T(512)S(6)} %compare.3, pred[]{:T(512)S(6)} %and.21), kind=kLoop, calls=%fused_computation.2.clone.1 | loop fusion | flops 18874368 | bytes 56623104 | tf_op jit(solution)/shard_map/while/body/eval_jaxpr/add | solution.py:119
  229.8 9.6 %collective-permute-done = bf16[64,9216]{1,0:T(8,128)(2,1)S(1)} collective-permute-done((bf16[64,9216]{1,0:T(8,128)(2,1)}, bf16[64,9216]{1,0:T(8,128)(2,1)S(1)}, u32[]{:S(2)}, u32[]{:S(2)}) %collective-permute-start) | collective-permute-done | bytes 1179680 | tf_op jit(solution)/shard_map/while/body/eval_jaxpr/ppermute | solution.py:14
  257.1 15.6 %fusion.58 = f32[9216,512]{0,1:T(8,128)} fusion(f32[9216,256]{0,1:T(8,128)S(1)} %fusion.56, f32[9216,256]{0,1:T(8,128)S(1)} %fusion.57, f32[9216,512]{0,1:T(8,128)} %get-tuple-element.546, pred[]{:T(512)S(6)} %compare.3, pred[]{:T(512)S(6)} %and.21), kind=kLoop, calls=%fused_computation.2.clone.1 | loop fusion | flops 18874368 | bytes 56623104 | tf_op jit(solution)/shard_map/while/body/eval_jaxpr/add | solution.py:119
  272.7 8.9 %collective-permute-done = bf16[64,9216]{1,0:T(8,128)(2,1)S(1)} collective-permute-done((bf16[64,9216]{1,0:T(8,128)(2,1)}, bf16[64,9216]{1,0:T(8,128)(2,1)S(1)}, u32[]{:S(2)}, u32[]{:S(2)}) %collective-permute-start) | collective-permute-done | bytes 1179680 | tf_op jit(solution)/shard_map/while/body/eval_jaxpr/ppermute | solution.py:14
  299.3 15.6 %fusion.58 = f32[9216,512]{0,1:T(8,128)} fusion(f32[9216,256]{0,1:T(8,128)S(1)} %fusion.56, f32[9216,256]{0,1:T(8,128)S(1)} %fusion.57, f32[9216,512]{0,1:T(8,128)} %get-tuple-element.546, pred[]{:T(512)S(6)} %compare.3, pred[]{:T(512)S(6)} %and.21), kind=kLoop, calls=%fused_computation.2.clone.1 | loop fusion | flops 18874368 | bytes 56623104 | tf_op jit(solution)/shard_map/while/body/eval_jaxpr/add | solution.py:119
  314.9 8.0 %collective-permute-done = bf16[64,9216]{1,0:T(8,128)(2,1)S(1)} collective-permute-done((bf16[64,9216]{1,0:T(8,128)(2,1)}, bf16[64,9216]{1,0:T(8,128)(2,1)S(1)}, u32[]{:S(2)}, u32[]{:S(2)}) %collective-permute-start) | collective-permute-done | bytes 1179680 | tf_op jit(solution)/shard_map/while/body/eval_jaxpr/ppermute | solution.py:14
  340.7 15.6 %fusion.58 = f32[9216,512]{0,1:T(8,128)} fusion(f32[9216,256]{0,1:T(8,128)S(1)} %fusion.56, f32[9216,256]{0,1:T(8,128)S(1)} %fusion.57, f32[9216,512]{0,1:T(8,128)} %get-tuple-element.546, pred[]{:T(512)S(6)} %compare.3, pred[]{:T(512)S(6)} %and.21), kind=kLoop, calls=%fused_computation.2.clone.1 | loop fusion | flops 18874368 | bytes 56623104 | tf_op jit(solution)/shard_map/while/body/eval_jaxpr/add | solution.py:119
  356.3 7.0 %collective-permute-done = bf16[64,9216]{1,0:T(8,128)(2,1)S(1)} collective-permute-done((bf16[64,9216]{1,0:T(8,128)(2,1)}, bf16[64,9216]{1,0:T(8,128)(2,1)S(1)}, u32[]{:S(2)}, u32[]{:S(2)}) %collective-permute-start) | collective-permute-done | bytes 1179680 | tf_op jit(solution)/shard_map/while/body/eval_jaxpr/ppermute | solution.py:14
  381.1 15.6 %fusion.58 = f32[9216,512]{0,1:T(8,128)} fusion(f32[9216,256]{0,1:T(8,128)S(1)} %fusion.56, f32[9216,256]{0,1:T(8,128)S(1)} %fusion.57, f32[9216,512]{0,1:T(8,128)} %get-tuple-element.546, pred[]{:T(512)S(6)} %compare.3, pred[]{:T(512)S(6)} %and.21), kind=kLoop, calls=%fused_computation.2.clone.1 | loop fusion | flops 18874368 | bytes 56623104 | tf_op jit(solution)/shard_map/while/body/eval_jaxpr/add | solution.py:119
  396.7 6.1 collective-permute-done
  420.6 15.6 %fusion.58 = f32[9216,512]{0,1:T(8,128)} fusion(f32[9216,256]{0,1:T(8,128)S(1)} %fusion.56, f32[9216,256]{0,1:T(8,128)S(1)} %fusion.57, f32[9216,512]{0,1:T(8,128)} %get-tuple-element.546, pred[]{:T(512)S(6)} %compare.3, pred[]{:T(512)S(6)} %and.21), kind=kLoop, calls=%fused_computation.2.clone.1 | loop fusion | flops 18874368 | bytes 56623104 | tf_op jit(solution)/shard_map/while/body/eval_jaxpr/add | solution.py:119
  436.2 5.2 collective-permute-done
  459.2 15.6 %fusion.58 = f32[9216,512]{0,1:T(8,128)} fusion(f32[9216,256]{0,1:T(8,128)S(1)} %fusion.56, f32[9216,256]{0,1:T(8,128)S(1)} %fusion.57, f32[9216,512]{0,1:T(8,128)} %get-tuple-element.546, pred[]{:T(512)S(6)} %compare.3, pred[]{:T(512)S(6)} %and.21), kind=kLoop, calls=%fused_computation.2.clone.1 | loop fusion | flops 18874368 | bytes 56623104 | tf_op jit(solution)/shard_map/while/body/eval_jaxpr/add | solution.py:119
  496.8 15.6 %fusion.58 = f32[9216,512]{0,1:T(8,128)} fusion(f32[9216,256]{0,1:T(8,128)S(1)} %fusion.56, f32[9216,256]{0,1:T(8,128)S(1)} %fusion.57, f32[9216,512]{0,1:T(8,128)} %get-tuple-element.546, pred[]{:T(512)S(6)} %compare.3, pred[]{:T(512)S(6)} %and.21), kind=kLoop, calls=%fused_computation.2.clone.1 | loop fusion | flops 18874368 | bytes 56623104 | tf_op jit(solution)/shard_map/while/body/eval_jaxpr/add | solution.py:119
  515.8 18.7 %copy.11 = f32[9216,512]{1,0:T(8,128)} copy(f32[9216,512]{0,1:T(8,128)} %get-tuple-element.326) | data formatting | bytes 37748736 | tf_op jit(solution)/shard_map/while | solution.py:128
  534.5 12.1 %multiply_convert_fusion = bf16[9216,512]{1,0:T(8,128)(2,1)} fusion(f32[9216,512]{1,0:T(8,128)} %copy.11), kind=kLoop, calls=%fused_computation.20 | loop fusion | flops 9437184 | bytes 28311552 | tf_op jit(solution)/shard_map/convert_element_type | solution.py:133
  546.6 139.0 %reduce-scatter.2.cloned.1.call-done = bf16[288,512]{1,0:T(8,128)(2,1)} async-done(((bf16[9216,512]{1,0:T(8,128)(2,1)}), bf16[288,512]{1,0:T(8,128)(2,1)}) %reduce-scatter.2.cloned.1.call-update) | async-done | bytes 294928 | tf_op jit(solution)/shard_map/reduce_scatter | solution.py:132
  (263 shorter events, 180.3 us)
Async XLA Ops:
  7.2 74.9 %all-gather.7.cloned.1.call-start = ((), (), s32[]{:S(2)}) async-start(), calls=%async_computation.3 | async-start | bytes 4866048 | tf_op jit(solution)/shard_map/all_gather | solution.py:79
  7.9 143.5 %all-gather.5.cloned.1.call-start = ((), (), s32[]{:S(2)}) async-start(), calls=%async_computation.2 | async-start | bytes 4866048 | tf_op jit(solution)/shard_map/all_gather | solution.py:80
  8.7 677.0 %reduce-scatter.2.cloned.1.call-start = ((), (), s32[]{:S(2)}) async-start(), calls=%async_computation.1 | async-start | bytes 9732096 | tf_op jit(solution)/shard_map/reduce_scatter | solution.py:132
  165.5 30.9 %collective-permute-start = (bf16[64,9216]{1,0:T(8,128)(2,1)}, bf16[64,9216]{1,0:T(8,128)(2,1)S(1)}, u32[]{:S(2)}, u32[]{:S(2)}) collective-permute-start(bf16[64,9216]{1,0:T(8,128)(2,1)} %get-tuple-element.521), channel_id=1, source_target_pairs={{32,0},{64,32},{96,64},{128,96},{160,128},{192,160},{224,192},{33,... | collective-permute-start | bytes 3538952 | tf_op jit(solution)/shard_map/while/body/eval_jaxpr/ppermute | solution.py:14
  170.9 25.5 %copy-start.5 = (bf16[128,9216]{1,0:T(8,128)(2,1)S(1)}, bf16[128,9216]{1,0:T(8,128)(2,1)}, u32[]{:S(2)}) copy-start(bf16[128,9216]{1,0:T(8,128)(2,1)} %copy-done.4) | copy-start | bytes 7077892 | tf_op jit(solution)/shard_map/while
  197.8 5.1 copy-start.3
  208.7 30.6 %collective-permute-start = (bf16[64,9216]{1,0:T(8,128)(2,1)}, bf16[64,9216]{1,0:T(8,128)(2,1)S(1)}, u32[]{:S(2)}, u32[]{:S(2)}) collective-permute-start(bf16[64,9216]{1,0:T(8,128)(2,1)} %get-tuple-element.521), channel_id=1, source_target_pairs={{32,0},{64,32},{96,64},{128,96},{160,128},{192,160},{224,192},{33,... | collective-permute-start | bytes 3538952 | tf_op jit(solution)/shard_map/while/body/eval_jaxpr/ppermute | solution.py:14
  214.1 25.2 %copy-start.5 = (bf16[128,9216]{1,0:T(8,128)(2,1)S(1)}, bf16[128,9216]{1,0:T(8,128)(2,1)}, u32[]{:S(2)}) copy-start(bf16[128,9216]{1,0:T(8,128)(2,1)} %copy-done.4) | copy-start | bytes 7077892 | tf_op jit(solution)/shard_map/while
  251.6 29.9 %collective-permute-start = (bf16[64,9216]{1,0:T(8,128)(2,1)}, bf16[64,9216]{1,0:T(8,128)(2,1)S(1)}, u32[]{:S(2)}, u32[]{:S(2)}) collective-permute-start(bf16[64,9216]{1,0:T(8,128)(2,1)} %get-tuple-element.521), channel_id=1, source_target_pairs={{32,0},{64,32},{96,64},{128,96},{160,128},{192,160},{224,192},{33,... | collective-permute-start | bytes 3538952 | tf_op jit(solution)/shard_map/while/body/eval_jaxpr/ppermute | solution.py:14
  257.1 24.5 %copy-start.5 = (bf16[128,9216]{1,0:T(8,128)(2,1)S(1)}, bf16[128,9216]{1,0:T(8,128)(2,1)}, u32[]{:S(2)}) copy-start(bf16[128,9216]{1,0:T(8,128)(2,1)} %copy-done.4) | copy-start | bytes 7077892 | tf_op jit(solution)/shard_map/while
  293.9 29.0 %collective-permute-start = (bf16[64,9216]{1,0:T(8,128)(2,1)}, bf16[64,9216]{1,0:T(8,128)(2,1)S(1)}, u32[]{:S(2)}, u32[]{:S(2)}) collective-permute-start(bf16[64,9216]{1,0:T(8,128)(2,1)} %get-tuple-element.521), channel_id=1, source_target_pairs={{32,0},{64,32},{96,64},{128,96},{160,128},{192,160},{224,192},{33,... | collective-permute-start | bytes 3538952 | tf_op jit(solution)/shard_map/while/body/eval_jaxpr/ppermute | solution.py:14
  299.3 23.6 %copy-start.5 = (bf16[128,9216]{1,0:T(8,128)(2,1)S(1)}, bf16[128,9216]{1,0:T(8,128)(2,1)}, u32[]{:S(2)}) copy-start(bf16[128,9216]{1,0:T(8,128)(2,1)} %copy-done.4) | copy-start | bytes 7077892 | tf_op jit(solution)/shard_map/while
  335.2 28.1 %collective-permute-start = (bf16[64,9216]{1,0:T(8,128)(2,1)}, bf16[64,9216]{1,0:T(8,128)(2,1)S(1)}, u32[]{:S(2)}, u32[]{:S(2)}) collective-permute-start(bf16[64,9216]{1,0:T(8,128)(2,1)} %get-tuple-element.521), channel_id=1, source_target_pairs={{32,0},{64,32},{96,64},{128,96},{160,128},{192,160},{224,192},{33,... | collective-permute-start | bytes 3538952 | tf_op jit(solution)/shard_map/while/body/eval_jaxpr/ppermute | solution.py:14
  340.7 22.7 %copy-start.5 = (bf16[128,9216]{1,0:T(8,128)(2,1)S(1)}, bf16[128,9216]{1,0:T(8,128)(2,1)}, u32[]{:S(2)}) copy-start(bf16[128,9216]{1,0:T(8,128)(2,1)} %copy-done.4) | copy-start | bytes 7077892 | tf_op jit(solution)/shard_map/while
  364.7 5.1 copy-start.3
  375.7 27.2 %collective-permute-start = (bf16[64,9216]{1,0:T(8,128)(2,1)}, bf16[64,9216]{1,0:T(8,128)(2,1)S(1)}, u32[]{:S(2)}, u32[]{:S(2)}) collective-permute-start(bf16[64,9216]{1,0:T(8,128)(2,1)} %get-tuple-element.521), channel_id=1, source_target_pairs={{32,0},{64,32},{96,64},{128,96},{160,128},{192,160},{224,192},{33,... | collective-permute-start | bytes 3538952 | tf_op jit(solution)/shard_map/while/body/eval_jaxpr/ppermute | solution.py:14
  381.1 21.7 %copy-start.5 = (bf16[128,9216]{1,0:T(8,128)(2,1)S(1)}, bf16[128,9216]{1,0:T(8,128)(2,1)}, u32[]{:S(2)}) copy-start(bf16[128,9216]{1,0:T(8,128)(2,1)} %copy-done.4) | copy-start | bytes 7077892 | tf_op jit(solution)/shard_map/while
  415.2 26.2 %collective-permute-start = (bf16[64,9216]{1,0:T(8,128)(2,1)}, bf16[64,9216]{1,0:T(8,128)(2,1)S(1)}, u32[]{:S(2)}, u32[]{:S(2)}) collective-permute-start(bf16[64,9216]{1,0:T(8,128)(2,1)} %get-tuple-element.521), channel_id=1, source_target_pairs={{32,0},{64,32},{96,64},{128,96},{160,128},{192,160},{224,192},{33,... | collective-permute-start | bytes 3538952 | tf_op jit(solution)/shard_map/while/body/eval_jaxpr/ppermute | solution.py:14
  420.6 20.8 %copy-start.5 = (bf16[128,9216]{1,0:T(8,128)(2,1)S(1)}, bf16[128,9216]{1,0:T(8,128)(2,1)}, u32[]{:S(2)}) copy-start(bf16[128,9216]{1,0:T(8,128)(2,1)} %copy-done.4) | copy-start | bytes 7077892 | tf_op jit(solution)/shard_map/while
  453.7 25.3 %collective-permute-start = (bf16[64,9216]{1,0:T(8,128)(2,1)}, bf16[64,9216]{1,0:T(8,128)(2,1)S(1)}, u32[]{:S(2)}, u32[]{:S(2)}) collective-permute-start(bf16[64,9216]{1,0:T(8,128)(2,1)} %get-tuple-element.521), channel_id=1, source_target_pairs={{32,0},{64,32},{96,64},{128,96},{160,128},{192,160},{224,192},{33,... | collective-permute-start | bytes 3538952 | tf_op jit(solution)/shard_map/while/body/eval_jaxpr/ppermute | solution.py:14
  459.1 19.9 %copy-start.5 = (bf16[128,9216]{1,0:T(8,128)(2,1)S(1)}, bf16[128,9216]{1,0:T(8,128)(2,1)}, u32[]{:S(2)}) copy-start(bf16[128,9216]{1,0:T(8,128)(2,1)} %copy-done.4) | copy-start | bytes 7077892 | tf_op jit(solution)/shard_map/while
  491.4 24.4 %collective-permute-start = (bf16[64,9216]{1,0:T(8,128)(2,1)}, bf16[64,9216]{1,0:T(8,128)(2,1)S(1)}, u32[]{:S(2)}, u32[]{:S(2)}) collective-permute-start(bf16[64,9216]{1,0:T(8,128)(2,1)} %get-tuple-element.521), channel_id=1, source_target_pairs={{32,0},{64,32},{96,64},{128,96},{160,128},{192,160},{224,192},{33,... | collective-permute-start | bytes 3538952 | tf_op jit(solution)/shard_map/while/body/eval_jaxpr/ppermute | solution.py:14
  496.8 19.0 %copy-start.5 = (bf16[128,9216]{1,0:T(8,128)(2,1)S(1)}, bf16[128,9216]{1,0:T(8,128)(2,1)}, u32[]{:S(2)}) copy-start(bf16[128,9216]{1,0:T(8,128)(2,1)} %copy-done.4) | copy-start | bytes 7077892 | tf_op jit(solution)/shard_map/while
  546.6 140.9 %copy-start.1 = (bf16[1,2,64,9216]{3,2,1,0:T(8,128)(2,1)S(1)}, bf16[1,2,64,9216]{3,2,1,0:T(8,128)(2,1)}, u32[]{:S(2)}) copy-start(bf16[1,2,64,9216]{3,2,1,0:T(8,128)(2,1)} %param.11) | copy-start | bytes 7077892
  (66 other events, 202.2 us)
Sparse Core Ops, SparseCore 0:
  9.9 72.1 all-gather.6
  84.0 67.4 all-gather.4
  546.7 138.8 reduce-scatter.1
where the time goes:
time: 697 us; the launch traced here: 694 us
  waiting for transfers between devices  333 us (48%)
  other arithmetic  193 us (28%)
  matrix products  86.4 us (12%)
  local copies, waits for them, and re-layouts  55.3 us (8%)
  between operations  13.8 us (2%)
  starting transfers between devices  11.6 us (2%)
    reduce_scatter x1, waiting for transfers between devices, per_device(): lax.psum_scatter((carry[2] / float(tok_count)).astype(jnp.bfloat16), 'rep...  139 us
    add x9, other arithmetic, advance(): running = running + jnp.where(active, terms, 0.0)  133 us
    ppermute x9, waiting for transfers between devices, from_behind(): lax.ppermute(value, axis, [(source, source + steps) for source in range(l...  69.6 us
    all_gather x1, waiting for transfers between devices, per_device(): lax.all_gather(up_weight[0], 'rep', axis=0, tiled=True)  65.5 us
    all_gather x1, waiting for transfers between devices, per_device(): lax.all_gather(down_weight[0], 'rep', axis=0, tiled=True)  57 us
    dot_general x18, matrix products, contract_rows(): lax.dot_general(left, right, (((0,), (0,)), ((), ())), preferred_element_...  37 us
    while x144, local copies, waits for them, and re-layouts  30.9 us
    dot_general x9, matrix products, advance(): jnp.dot(out_grad, w_up, preferred_element_type=jnp.float32) * slope_rows  30.4 us
  transfers between devices with their start and end apart: 12, of which 12 were waited for; matrix products, arithmetic and copies ran while one was open for 27% of the time, Pallas kernels for 0%

commit v1 on v0

v1 whole, which is shorter than its diff:
```python
import jax
import jax.numpy as jnp
from jax import lax
from jax.experimental import pallas as pl
from jax.experimental.pallas import tpu as pltpu
from jax.sharding import PartitionSpec as P

EPSILON = 1e-05
HALF_ROOT = 0.7071067811865476
DENSITY = 0.3989422804014327
MESH = pl.DeviceIdType.MESH

D = 9216
R = 256
TOK = 64
ROWS = 128
NSEC = 8
NZ = 8
QUAD = D // NZ
SHARD = QUAD // 4
HALF = SHARD // 2
BLK = 16
NBLK = ROWS // BLK
NCH = 4
CHW = D // NCH
QPC = NZ // NCH
ECH = 8
ECW = D // ECH
NSEM = 160
F32 = jnp.float32
BF16 = jnp.bfloat16


def nn(left, right):
    return lax.dot_general(left, right, (((1,), (0,)), ((), ())), preferred_element_type=F32)


def nt(left, right):
    return lax.dot_general(left, right, (((1,), (1,)), ((), ())), preferred_element_type=F32)


def tn(left, right):
    return lax.dot_general(left, right, (((0,), (0,)), ((), ())), preferred_element_type=F32)


def kernel(
    hist_h, codes_h, scales, ids, cot_h, gain, bias, wd_h, wu_h,
    ig_h, ag_h,
    hist, codes, xin, norm, wd, wu, grad, res,
    acc, slopes, qmat, ugain, hidden, acts, mean_s, inv_s, scol,
    pd, pu, qd, qu, xsend, xrecv, su, ru, sd, rd, usend, urecv, final,
    ss, rs, css, crs, osem, lsem,
):
    sec = lax.axis_index("section")
    rep = lax.axis_index("rep")
    z = rep // 4
    xl = (rep // 2) % 2
    core = rep % 2
    oxl = 1 - xl
    ocore = 1 - core

    def zi(step):
        return (z + step + NZ) % NZ

    def at_z(step):
        return (sec, zi(step) * 4 + xl * 2 + core)

    up, down = at_z(1), at_z(-1)
    side = (sec, z * 4 + oxl * 2 + core)
    twin = (sec, z * 4 + xl * 2 + ocore)
    below = (jnp.maximum(sec - 1, 0), rep)
    above = (jnp.minimum(sec + 1, NSEC - 1), rep)

    names = {}
    pending = []

    def sid(name):
        return names.setdefault(name, len(names))

    def link(name, src, dst, device):
        index = sid(name)
        return pltpu.make_async_remote_copy(
            src_ref=src, dst_ref=dst, send_sem=ss.at[index], recv_sem=rs.at[index],
            device_id=device, device_id_type=MESH,
        )

    def put(name, src, dst, device):
        copy = link(name, src, dst, device)
        copy.start()
        pending.append(copy)

    def got(name, dst, device):
        link(name, dst, dst, device).wait_recv()

    loads = [
        pltpu.make_async_copy(hist_h.at[0], hist, lsem.at[0]),
        pltpu.make_async_copy(codes_h.at[0], codes, lsem.at[1]),
        pltpu.make_async_copy(wd_h.at[0], wd.at[z, xl, core], lsem.at[2]),
        pltpu.make_async_copy(wu_h.at[0], wu.at[z, xl, core], lsem.at[3]),
    ]
    for load in loads:
        load.start()

    def seed(m):
        return pltpu.make_async_copy(cot_h.at[m], grad.at[pl.ds(m * TOK, TOK)], lsem.at[4 + m])

    @pl.when(sec == NSEC - 1)
    def _():
        for m in range(2):
            seed(m).start()

    barrier = pltpu.get_barrier_semaphore()
    for device in (up, down, side, twin):
        pl.semaphore_signal(barrier, inc=1, device_id=device, device_id_type=MESH)

    @pl.when(sec > 0)
    def _():
        pl.semaphore_signal(barrier, inc=1, device_id=below, device_id_type=MESH)

    @pl.when(sec < NSEC - 1)
    def _():
        pl.semaphore_signal(barrier, inc=1, device_id=above, device_id_type=MESH)

    @pl.when((sec > 0) & (sec < NSEC - 1))
    def _():
        pl.semaphore_wait(barrier, 6)

    @pl.when((sec == 0) | (sec == NSEC - 1))
    def _():
        pl.semaphore_wait(barrier, 5)

    own_d, own_u = wd.at[z, xl, core], wu.at[z, xl, core]
    put("Ux0", wu_h.at[0], own_u, side)
    put("Dz+0", wd_h.at[0], own_d, up)
    put("Dz-0", wd_h.at[0], own_d, down)
    put("Uz+0s", wu_h.at[0], own_u, up)
    put("Uz-0s", wu_h.at[0], own_u, down)
    put("Dx0", wd_h.at[0], own_d, side)
    put("Ds0", wd_h.at[0], own_d, twin)
    put("Us0", wu_h.at[0], own_u, twin)

    for load in loads[:2]:
        load.wait()

    eye = (
        lax.broadcasted_iota(jnp.int32, (TOK, TOK), 0)
        == lax.broadcasted_iota(jnp.int32, (TOK, TOK), 1)
    )
    for m in range(2):
        row = scales[0, pl.ds(m, 1), :]
        scol[pl.ds(m * TOK, TOK), :] = jnp.sum(
            jnp.where(eye, row, 0.0), axis=1, keepdims=True
        )

    def rebuild(i):
        rows = pl.ds(pl.multiple_of(i * BLK, BLK), BLK)
        m = i // (TOK // BLK)
        inner = pl.ds(pl.multiple_of((i % (TOK // BLK)) * BLK, BLK), BLK)
        step = scol[rows, :]
        pick = ids[0, m]
        total = jnp.zeros((BLK, 1), F32)
        for e in range(ECH):
            cols = pl.ds(e * ECW, ECW)
            value = hist[pick, inner, cols].astype(F32) + step * codes[m, inner, cols].astype(F32)
            value = value.astype(BF16)
            xin[rows, cols] = value
            total = total + jnp.sum(value.astype(F32), axis=1, keepdims=True)
        mean = total * (1.0 / D)
        square = jnp.zeros((BLK, 1), F32)
        for e in range(ECH):
            cols = pl.ds(e * ECW, ECW)
            centred = xin[rows, cols].astype(F32) - mean
            square = square + jnp.sum(centred * centred, axis=1, keepdims=True)
        inv = lax.rsqrt(square * (1.0 / D) + EPSILON)
        mean_s[rows, :] = mean
        inv_s[rows, :] = inv
        for e in range(ECH):
            cols = pl.ds(e * ECW, ECW)
            scaled = (xin[rows, cols].astype(F32) - mean) * inv
            norm[rows, cols] = (scaled * gain[:, cols] + bias[:, cols]).astype(BF16)

    def rebuild_some(first, count):
        def step(i, carry):
            rebuild(first + i)
            return carry

        lax.fori_loop(0, count, step, 0)

    def extra_rows():
        line = lax.broadcasted_iota(jnp.int32, (BLK, ECW), 0)
        for e in range(ECH):
            cols = pl.ds(e * ECW, ECW)
            g, b = gain[:, cols], bias[:, cols]
            g_hi, b_hi = g.astype(BF16).astype(F32), b.astype(BF16).astype(F32)
            stack = jnp.where(line == 0, g_hi, 0.0)
            stack = jnp.where(line == 1, g - g_hi, stack)
            stack = jnp.where(line == 2, b_hi, stack)
            stack = jnp.where(line == 3, b - b_hi, stack)
            norm[pl.ds(ROWS, BLK), cols] = stack.astype(BF16)

    def quad_cols(q):
        return pl.ds(pl.multiple_of(q * QUAD, QUAD), QUAD)

    def forward(q, first=False):
        part = nn(norm[:, quad_cols(q)], wd[q].reshape(QUAD, R))
        if first:
            acc[...] = part
        else:
            acc[...] += part

    extra_rows()
    got("Ux0", wu.at[z, oxl, core], side)
    put("Uz+0p", wu.at[z, oxl, core], wu.at[z, oxl, core], up)
    put("Uz-0p", wu.at[z, oxl, core], wu.at[z, oxl, core], down)
    put("Uxs0", wu.at[z, oxl, core], wu.at[z, oxl, core], twin)
    got("Dx0", wd.at[z, oxl, core], side)
    put("Dxs0", wd.at[z, oxl, core], wd.at[z, oxl, core], twin)
    rebuild_some(0, 2)

    def piece(ref, direction, dist, e, c):
        q = zi(-dist if direction == "+" else dist)
        if dist < 4 or ref is wu:
            return ref.at[q, e, c]
        first = 0 if direction == "+" else HALF
        return ref.at[q, e, c, pl.ds(first, HALF)]

    def onward(ref, direction, dist, e, c):
        q = zi(-dist if direction == "+" else dist)
        if dist < 3 or ref is wu:
            return ref.at[q, e, c]
        first = 0 if direction == "+" else HALF
        return ref.at[q, e, c, pl.ds(first, HALF)]

    ways = (("+", up, down), ("-", down, up))

    def down_ready(dist):
        if dist == 0:
            got("Ds0", wd.at[z, xl, ocore], twin)
            got("Dxs0", wd.at[z, oxl, ocore], twin)
            return
        for way, _, _ in ways:
            got(f"Ds{way}{dist}", piece(wd, way, dist, xl, ocore), twin)
            got(f"Dxs{way}{dist}", piece(wd, way, dist, oxl, ocore), twin)

    for dist in range(1, 5):
        for way, ahead, behind in ways:
            part = piece(wd, way, dist, xl, core)
            got(f"Dz{way}{dist - 1}", part, behind)
            if dist < 4:
                more = onward(wd, way, dist, xl, core)
                put(f"Dz{way}{dist}", more, more, ahead)
            put(f"Dx{way}{dist}", part, part, side)
            put(f"Ds{way}{dist}", part, part, twin)
        for which, e in (("s", xl), ("p", oxl)):
            for way, ahead, behind in ways:
                if dist == 4 and (way == "+") != (which == "s"):
                    continue
                part = piece(wu, way, dist, e, core)
                got(f"Uz{way}{dist - 1}{which}", part, behind)
                if dist < 3 or (dist == 3 and (way == "+") == (which == "s")):
                    put(f"Uz{way}{dist}{which}", part, part, ahead)
                put(f"Us{way}{dist}{which}", part, part, twin)
        for way, ahead, behind in ways:
            part = piece(wd, way, dist, oxl, core)
            got(f"Dx{way}{dist}", part, side)
            put(f"Dxs{way}{dist}", part, part, twin)
        if dist < 4:
            rebuild_some(2 * dist, 2)
        if dist == 3:
            loads[2].wait()
            down_ready(0)
            forward(zi(0), True)
            down_ready(1)
            forward(zi(-1))
            forward(zi(1))
    for dist in (2, 3):
        down_ready(dist)
        forward(zi(-dist))
        forward(zi(dist))
    down_ready(4)
    forward(zi(4))

    shift = acc[ROWS + 2 : ROWS + 3, :] + acc[ROWS + 3 : ROWS + 4, :]
    ugain[...] = acc[ROWS : ROWS + 1, :] + acc[ROWS + 1 : ROWS + 2, :]
    for i in range(4):
        rows = pl.ds(i * 32, 32)
        preact = acc[rows, :]
        cdf = 0.5 * (1.0 + lax.erf(preact * HALF_ROOT))
        bump = DENSITY * jnp.exp(-0.5 * preact * preact)
        hidden[rows, :] = (preact * cdf).astype(BF16)
        slopes[rows, :] = cdf + preact * bump
        qmat[rows, :] = preact - shift

    loads[3].wait()
    got("Us0", wu.at[z, xl, ocore], twin)
    got("Uxs0", wu.at[z, oxl, ocore], twin)
    for dist in range(1, 5):
        for which, e in (("s", xl), ("p", oxl)):
            for way, _, _ in ways:
                if dist == 4 and (way == "+") != (which == "s"):
                    continue
                got(f"Us{way}{dist}{which}", piece(wu, way, dist, e, ocore), twin)

    @pl.when(sec == NSEC - 1)
    def _():
        for m in range(2):
            seed(m).wait()

    def hop(i, ch, src):
        rows = pl.ds(pl.multiple_of(i * BLK, BLK), BLK)
        index = i * NCH + ch
        return pltpu.make_async_remote_copy(
            src_ref=src.at[rows, pl.ds(ch * CHW, CHW)],
            dst_ref=grad.at[rows, pl.ds(ch * CHW, CHW)],
            send_sem=css.at[index], recv_sem=crs.at[index],
            device_id=below, device_id_type=MESH,
        )

    def keep(i):
        inner = pl.ds(pl.multiple_of((i % (TOK // BLK)) * BLK, BLK), BLK)
        rows = pl.ds(pl.multiple_of(i * BLK, BLK), BLK)
        return pltpu.make_async_copy(
            res.at[rows], ig_h.at[0, i // (TOK // BLK), inner], osem.at[i]
        )

    def chain(i, carry):
        rows = pl.ds(pl.multiple_of(i * BLK, BLK), BLK)
        lift = jnp.zeros((BLK, R), F32)
        for ch in range(NCH):
            @pl.when(sec < NSEC - 1)
            def _():
                hop(i, ch, grad).wait_recv()

            lift = lift + nn(
                grad[rows, ch * CHW : (ch + 1) * CHW],
                wu[ch * QPC : (ch + 1) * QPC].reshape(CHW, R),
            )
        act = (lift * slopes[rows, :]).astype(BF16)
        acts[rows, :] = act
        wide = act.astype(F32)
        m1 = jnp.sum(wide * ugain[...], axis=1, keepdims=True) * (1.0 / D)
        m2 = jnp.sum(wide * qmat[rows, :], axis=1, keepdims=True) * (1.0 / D)
        mean, inv = mean_s[rows, :], inv_s[rows, :]
        tilt = inv * inv * m2
        base = inv * m1 - mean * tilt
        for ch in range(NCH):
            cols = pl.ds(ch * CHW, CHW)
            back = nt(act, wd[ch * QPC : (ch + 1) * QPC].reshape(CHW, R))
            value = (
                grad[rows, cols].astype(F32) + inv * (back * gain[:, cols]) - base
                - xin[rows, cols].astype(F32) * tilt
            )
            res[rows, cols] = value.astype(BF16)

            @pl.when(sec > 0)
            def _():
                hop(i, ch, res).start()

        keep(i).start()
        return carry

    lax.fori_loop(0, NBLK, chain, 0)

    def terms(q):
        cols = quad_cols(q)
        pd[q] = (tn(norm[:ROWS, cols], acts[...]) * (1.0 / TOK)).astype(BF16).reshape(2, 2, SHARD, R)
        pu[q] = (tn(grad[:, cols], hidden[...]) * (1.0 / TOK)).astype(BF16).reshape(2, 2, SHARD, R)

    def make(step):
        q = zi(step)
        terms(q)
        put(f"Pu{step}", pu.at[q, :, ocore], qu.at[q], twin)
        put(f"Pd{step}", pd.at[q, :, ocore], qd.at[q], twin)

    def heard(step):
        q = zi(step)
        got(f"Pu{step}", qu.at[q], twin)
        got(f"Pd{step}", qd.at[q], twin)

    def cross(step):
        q = zi(step)
        xsend[q] = (pd[q, oxl, core].astype(F32) + qd[q, oxl].astype(F32)).astype(BF16)
        put(f"X{step}", xsend.at[q], xrecv.at[q], side)

    def send_up_half(j):
        dist = 4 - j
        for way, ahead, behind in ways:
            d = 0 if way == "+" else 1
            q = zi(dist if way == "+" else -dist)
            order = ("p", "s") if way == "+" else ("s", "p")
            for which in order:
                lead = (way == "+") == (which == "s")
                if j == 0 and not lead:
                    continue
                e, k = (xl, 0) if which == "s" else (oxl, 1)
                value = pu[q, e, core].astype(F32) + qu[q, e].astype(F32)
                if j >= 2 or (j == 1 and lead):
                    got(f"RU{way}{j - 1}{which}", ru.at[d, j - 1, k], behind)
                    value = value + ru[d, j - 1, k].astype(F32)
                su[d, j, k] = value.astype(BF16)
                put(f"RU{way}{j}{which}", su.at[d, j, k], ru.at[d, j, k], ahead)

    def send_down_half(j):
        dist = 4 - j
        if j == 0:
            got("X4", xrecv.at[zi(4)], side)
        else:
            for way, _, _ in ways:
                step = dist if way == "+" else -dist
                got(f"X{step}", xrecv.at[zi(step)], side)
        for way, ahead, behind in ways:
            d = 0 if way == "+" else 1
            q = zi(dist if way == "+" else -dist)
            part = pl.ds(0 if way == "+" else HALF, HALF)
            if j == 0:
                value = (
                    pd[q, xl, core, part].astype(F32) + qd[q, xl, part].astype(F32)
                    + xrecv[q, part].astype(F32)
                )
                sd[d, 0, part] = value.astype(BF16)
                put(f"RD{way}0", sd.at[d, 0, part], rd.at[d, 0, part], ahead)
                continue
            value = (
                pd[q, xl, core].astype(F32) + qd[q, xl].astype(F32) + xrecv[q].astype(F32)
            )
            sd[d, j] = value.astype(BF16)
            if j == 1:
                got(f"RD{way}0", rd.at[d, 0, part], behind)
                sd[d, j, part] = (
                    pd[q, xl, core, part].astype(F32) + qd[q, xl, part].astype(F32)
                    + xrecv[q, part].astype(F32) + rd[d, 0, part].astype(F32)
                ).astype(BF16)
            else:
                got(f"RD{way}{j - 1}", rd.at[d, j - 1], behind)
                sd[d, j] = (value + rd[d, j - 1].astype(F32)).astype(BF16)
            put(f"RD{way}{j}", sd.at[d, j], rd.at[d, j], ahead)

    make(4)
    make(3)
    make(-3)
    heard(4)
    send_up_half(0)
    cross(4)
    make(2)
    make(-2)
    heard(3)
    heard(-3)
    send_up_half(1)
    cross(3)
    cross(-3)
    make(1)
    make(-1)
    send_down_half(0)
    make(0)
    heard(2)
    heard(-2)
    send_up_half(2)
    cross(2)
    cross(-2)
    heard(1)
    heard(-1)
    cross(1)
    cross(-1)
    heard(0)
    cross(0)
    send_down_half(1)
    send_up_half(3)
    send_down_half(2)
    for way, _, behind in ways:
        d = 0 if way == "+" else 1
        got(f"RU{way}3p", ru.at[d, 3, 1], behind)
    usend[...] = (
        pu[z, oxl, core].astype(F32) + qu[z, oxl].astype(F32)
        + ru[0, 3, 1].astype(F32) + ru[1, 3, 1].astype(F32)
    ).astype(BF16)
    put("UF", usend, urecv, side)
    send_down_half(3)
    for way, _, behind in ways:
        d = 0 if way == "+" else 1
        got(f"RU{way}3s", ru.at[d, 3, 0], behind)
    got("UF", urecv, side)
    final[:, pl.ds(R, R)] = (
        pu[z, xl, core].astype(F32) + qu[z, xl].astype(F32)
        + ru[0, 3, 0].astype(F32) + ru[1, 3, 0].astype(F32) + urecv[...].astype(F32)
    )
    got("X0", xrecv.at[z], side)
    for way, _, behind in ways:
        d = 0 if way == "+" else 1
        got(f"RD{way}3", rd.at[d, 3], behind)
    final[:, pl.ds(0, R)] = (
        pd[z, xl, core].astype(F32) + qd[z, xl].astype(F32) + xrecv[z].astype(F32)
        + rd[0, 3].astype(F32) + rd[1, 3].astype(F32)
    )
    store = pltpu.make_async_copy(final, ag_h.at[0], lsem.at[6])
    store.start()

    for copy in pending:
        copy.wait_send()

    def settle(i, carry):
        @pl.when(sec > 0)
        def _():
            for ch in range(NCH):
                hop(i, ch, res).wait_send()

        keep(i).wait()
        return carry

    lax.fori_loop(0, NBLK, settle, 0)
    store.wait()
    assert len(names) <= NSEM


def per_device(*arrays):
    vmem = pl.BlockSpec(memory_space=pltpu.VMEM)
    smem = pl.BlockSpec(memory_space=pltpu.SMEM)
    hbm = pl.BlockSpec(memory_space=pl.ANY)
    return pl.pallas_call(
        kernel,
        out_shape=(
            jax.ShapeDtypeStruct((1, 2, TOK, D), BF16),
            jax.ShapeDtypeStruct((1, SHARD, 2 * R), F32),
        ),
        in_specs=[hbm, hbm, vmem, smem, hbm, vmem, vmem, hbm, hbm],
        out_specs=(hbm, hbm),
        scratch_shapes=[
            pltpu.VMEM((2, TOK, D), BF16),
            pltpu.VMEM((2, TOK, D), jnp.int32),
            pltpu.VMEM((ROWS, D), BF16),
            pltpu.VMEM((ROWS + BLK, D), BF16),
            pltpu.VMEM((NZ, 2, 2, SHARD, R), BF16),
            pltpu.VMEM((NZ, 2, 2, SHARD, R), BF16),
            pltpu.VMEM((ROWS, D), BF16),
            pltpu.VMEM((ROWS, D), BF16),
            pltpu.VMEM((ROWS + BLK, R), F32),
            pltpu.VMEM((ROWS, R), F32),
            pltpu.VMEM((ROWS, R), F32),
            pltpu.VMEM((1, R), F32),
            pltpu.VMEM((ROWS, R), BF16),
            pltpu.VMEM((ROWS, R), BF16),
            pltpu.VMEM((ROWS, 1), F32),
            pltpu.VMEM((ROWS, 1), F32),
            pltpu.VMEM((ROWS, 1), F32),
            pltpu.VMEM((NZ, 2, 2, SHARD, R), BF16),
            pltpu.VMEM((NZ, 2, 2, SHARD, R), BF16),
            pltpu.VMEM((NZ, 2, SHARD, R), BF16),
            pltpu.VMEM((NZ, 2, SHARD, R), BF16),
            pltpu.VMEM((NZ, SHARD, R), BF16),
            pltpu.VMEM((NZ, SHARD, R), BF16),
            pltpu.VMEM((2, 4, 2, SHARD, R), BF16),
            pltpu.VMEM((2, 4, 2, SHARD, R), BF16),
            pltpu.VMEM((2, 4, SHARD, R), BF16),
            pltpu.VMEM((2, 4, SHARD, R), BF16),
            pltpu.VMEM((SHARD, R), BF16),
            pltpu.VMEM((SHARD, R), BF16),
            pltpu.VMEM((SHARD, 2 * R), F32),
            pltpu.SemaphoreType.DMA((NSEM,)),
            pltpu.SemaphoreType.DMA((NSEM,)),
            pltpu.SemaphoreType.DMA((NBLK * NCH,)),
            pltpu.SemaphoreType.DMA((NBLK * NCH,)),
            pltpu.SemaphoreType.DMA((NBLK,)),
            pltpu.SemaphoreType.DMA((8,)),
        ],
        compiler_params=pltpu.CompilerParams(
            collective_id=0, has_side_effects=True, vmem_limit_bytes=60 << 20
        ),
        cost_estimate=pl.CostEstimate(
            flops=10 * ROWS * D * R, bytes_accessed=24 << 20, transcendentals=2 * ROWS * R
        ),
    )(*arrays)


def solution(mesh):
    return jax.shard_map(
        per_device,
        mesh=mesh,
        in_specs=(
            P("section", "rep", None, None),
            P("section", "rep", None, None),
            P("section", "rep", None),
            P("rep", None),
            P("rep", None, None),
            P("section", None),
            P("section", None),
            P("section", "rep", None),
            P("section", "rep", None),
        ),
        out_specs=(P("section", "rep", None, None), P("section", "rep", None)),
        check_vma=False,
    )
```

time: 697 us -> 212 us (0.30)
  waiting for transfers between devices: 333 us -> 0 us
  Pallas kernels: 0 us -> 207 us
  other arithmetic: 193 us -> 0 us
  matrix products: 86.4 us -> 0 us
  local copies, waits for them, and re-layouts: 55.3 us -> 4.1 us
  between operations: 13.8 us -> 0.65 us
  starting transfers between devices: 11.6 us -> 0 us
    pallas_call x0 -> x1, Pallas kernels: none -> 207 us  [per_device(): pl.pallas_call(kernel, out_shape=(jax.ShapeDtypeStruct((1, 2, TOK, D), BF...]
    reduce_scatter x1 -> x0, waiting for transfers between devices: 139 us -> none  [per_device(): lax.psum_scatter((carry[2] / float(tok_count)).astype(jnp.bfloat16), 'rep...]
    add x9 -> x0, other arithmetic: 133 us -> none  [advance(): running = running + jnp.where(active, terms, 0.0)]
    all_gather x2 -> x0, waiting for transfers between devices: 122 us -> none  [the longest x1 65.5 us: per_device(): lax.all_gather(up_weight[0], 'rep', axis=0, tiled=True)]
    dot_general x37 -> x0, matrix products: 86.4 us -> none  [the longest x18 37 us: contract_rows(): lax.dot_general(left, right, (((0,), (0,)), ((), ())), preferred_element_...]
    ppermute x9 -> x0, waiting for transfers between devices: 69.6 us -> none  [from_behind(): lax.ppermute(value, axis, [(source, source + steps) for source in range(l...]
    while x145 -> x0, local copies, waits for them, and re-layouts: 49.7 us -> none
    convert_element_type x2 -> x0, other arithmetic: 19.2 us -> none  [the longest x1 12.1 us: per_device(): (carry[2] / float(tok_count)).astype(jnp.bfloat16)]
  transfers between devices with their start and end apart: 12 -> 0, of which waited for: 12 -> 0; matrix products, arithmetic and copies ran while one was open for 27% -> 0% of each run, Pallas kernels for 0% -> 0%
where the time goes in v1:
time: 212 us
  Pallas kernels  207 us (98%)
  local copies, waits for them, and re-layouts  4.1 us (2%)
    pallas_call x1, Pallas kernels, per_device(): pl.pallas_call(kernel, out_shape=(jax.ShapeDtypeStruct((1, 2, TOK, D), BF...  207 us

profile of v1, /device:TPU:1, one launch (start us, length us, event | category | flops | bytes accessed | tf_op | source)
XLA Modules:
  0.0 211.6 jit_solution(2635781590164408926)
XLA Ops:
  0.6 206.9 %shard_map.104 = (bf16[1,2,64,9216]{3,2,1,0:T(8,128)(2,1)}, f32[1,288,512]{2,1,0:T(8,128)}) custom-call(bf16[1,2,64,9216]{3,2,1,0:T(8,128)(2,1)} %hist_h.1, s32[1,2,64,9216]{3,2,1,0:T(8,128)} %codes_h.1, f32[1,2,64]{2,1,0:T(2,128)} %scales.1, s32[1,2]{1,0:T(1,128)} %ids.1, bf16[2,64,9216]{2,1,0:T(8,128)(2,1)} %cot_h.1, f32[1,9216]{1,0:T(1,128)} %gain.1, ...), custom_call_target="tpu_custom_call" | custom-call | flops 3019898880 | bytes 25165824 | tf_op jit(solution)/shard_map/pallas_call | solution.py:518
  207.5 0.0 copy-start
  207.5 3.3 %copy.13 = bf16[1,2,64,9216]{3,2,1,0:T(8,128)(2,1)} copy(bf16[1,2,64,9216]{3,2,1,0:T(8,128)(2,1)} %get-tuple-element.4) | data formatting | bytes 4718592
  210.8 0.0 copy-done
  210.8 0.8 copy.14
Async XLA Ops:
  207.5 3.3 %copy-start = (f32[1,288,512]{2,1,0:T(8,128)S(1)}, f32[1,288,512]{2,1,0:T(8,128)}, u32[]{:S(2)}) copy-start(f32[1,288,512]{2,1,0:T(8,128)} %get-tuple-element.5) | copy-start | bytes 1769476

commit v2 on v1

--- a/solution.py
+++ b/solution.py
@@ -21,12 +21,9 @@
 HALF = SHARD // 2
 BLK = 16
 NBLK = ROWS // BLK
-NCH = 4
-CHW = D // NCH
-QPC = NZ // NCH
 ECH = 8
 ECW = D // ECH
-NSEM = 160
+NSEM = 96
 F32 = jnp.float32
 BF16 = jnp.bfloat16
 
@@ -48,8 +45,8 @@
     ig_h, ag_h,
     hist, codes, xin, norm, wd, wu, grad, res,
     acc, slopes, qmat, ugain, hidden, acts, mean_s, inv_s, scol,
-    pd, pu, qd, qu, xsend, xrecv, su, ru, sd, rd, usend, urecv, final,
-    ss, rs, css, crs, osem, lsem,
+    gather_n, gather_g, gather_h, gather_a, total, tsend, trecv, xsend, xrecv, final,
+    ss, rs, css, crs, gss, grs, ass, ars, osem, lsem,
 ):
     sec = lax.axis_index("section")
     rep = lax.axis_index("rep")
@@ -110,7 +107,8 @@
             seed(m).start()
 
     barrier = pltpu.get_barrier_semaphore()
-    for device in (up, down, side, twin):
+    ring = [at_z(step) for step in range(1, NZ)]
+    for device in (*ring, side, twin):
         pl.semaphore_signal(barrier, inc=1, device_id=device, device_id_type=MESH)
 
     @pl.when(sec > 0)
@@ -123,11 +121,11 @@
 
     @pl.when((sec > 0) & (sec < NSEC - 1))
     def _():
-        pl.semaphore_wait(barrier, 6)
+        pl.semaphore_wait(barrier, len(ring) + 4)
 
     @pl.when((sec == 0) | (sec == NSEC - 1))
     def _():
-        pl.semaphore_wait(barrier, 5)
+        pl.semaphore_wait(barrier, len(ring) + 3)
 
     own_d, own_u = wd.at[z, xl, core], wu.at[z, xl, core]
     put("Ux0", wu_h.at[0], own_u, side)
@@ -306,46 +304,86 @@
         for m in range(2):
             seed(m).wait()
 
-    def hop(i, ch, src):
-        rows = pl.ds(pl.multiple_of(i * BLK, BLK), BLK)
-        index = i * NCH + ch
+    for step in range(1, NZ):
+        q = zi(step)
+        put(f"N{step}", norm.at[pl.ds(0, ROWS), quad_cols(q)], gather_n.at[z], at_z(step))
+    own_n = pltpu.make_async_copy(
+        norm.at[pl.ds(0, ROWS), quad_cols(z)], gather_n.at[z], lsem.at[7]
+    )
+    own_n.start()
+    for step in range(1, NZ):
+        put(f"H{step}", hidden, gather_h.at[z], at_z(step))
+    gather_h[z] = hidden[...]
+
+    def rows_of(i):
+        return pl.ds(pl.multiple_of(i * BLK, BLK), BLK)
+
+    def hop(i, n, src):
+        part = (rows_of(i), quad_cols(zi(n + 1)))
+        index = i * NZ + n
         return pltpu.make_async_remote_copy(
-            src_ref=src.at[rows, pl.ds(ch * CHW, CHW)],
-            dst_ref=grad.at[rows, pl.ds(ch * CHW, CHW)],
+            src_ref=src.at[part], dst_ref=grad.at[part],
             send_sem=css.at[index], recv_sem=crs.at[index],
             device_id=below, device_id_type=MESH,
         )
 
+    def spread_grad(i, n, landing):
+        index = i * NZ + n
+        return pltpu.make_async_remote_copy(
+            src_ref=grad.at[rows_of(i), quad_cols(zi(n + 1))],
+            dst_ref=gather_g.at[landing, rows_of(i)],
+            send_sem=gss.at[index], recv_sem=grs.at[index],
+            device_id=at_z(n + 1), device_id_type=MESH,
+        )
+
+    def own_grad(i):
+        return pltpu.make_async_copy(
+            grad.at[rows_of(i), quad_cols(z)], gather_g.at[z, rows_of(i)],
+            grs.at[i * NZ + NZ - 1],
+        )
+
+    def spread_act(i, n, landing):
+        index = i * NZ + n
+        return pltpu.make_async_remote_copy(
+            src_ref=acts.at[rows_of(i)], dst_ref=gather_a.at[landing, rows_of(i)],
+            send_sem=ass.at[index], recv_sem=ars.at[index],
+            device_id=at_z(n + 1), device_id_type=MESH,
+        )
+
     def keep(i):
         inner = pl.ds(pl.multiple_of((i % (TOK // BLK)) * BLK, BLK), BLK)
-        rows = pl.ds(pl.multiple_of(i * BLK, BLK), BLK)
         return pltpu.make_async_copy(
-            res.at[rows], ig_h.at[0, i // (TOK // BLK), inner], osem.at[i]
+            res.at[rows_of(i)], ig_h.at[0, i // (TOK // BLK), inner], osem.at[i]
         )
 
     def chain(i, carry):
-        rows = pl.ds(pl.multiple_of(i * BLK, BLK), BLK)
+        rows = rows_of(i)
         lift = jnp.zeros((BLK, R), F32)
-        for ch in range(NCH):
+        for n in range(NZ):
+            q = zi(n + 1)
+
             @pl.when(sec < NSEC - 1)
             def _():
-                hop(i, ch, grad).wait_recv()
-
-            lift = lift + nn(
-                grad[rows, ch * CHW : (ch + 1) * CHW],
-                wu[ch * QPC : (ch + 1) * QPC].reshape(CHW, R),
-            )
+                hop(i, n, grad).wait_recv()
+
+            if n < NZ - 1:
+                spread_grad(i, n, z).start()
+            else:
+                own_grad(i).start()
+            lift = lift + nn(grad[rows, quad_cols(q)], wu[q].reshape(QUAD, R))
         act = (lift * slopes[rows, :]).astype(BF16)
         acts[rows, :] = act
+        gather_a[z, rows, :] = act
         wide = act.astype(F32)
         m1 = jnp.sum(wide * ugain[...], axis=1, keepdims=True) * (1.0 / D)
         m2 = jnp.sum(wide * qmat[rows, :], axis=1, keepdims=True) * (1.0 / D)
         mean, inv = mean_s[rows, :], inv_s[rows, :]
         tilt = inv * inv * m2
         base = inv * m1 - mean * tilt
-        for ch in range(NCH):
-            cols = pl.ds(ch * CHW, CHW)
-            back = nt(act, wd[ch * QPC : (ch + 1) * QPC].reshape(CHW, R))
+        for n in range(NZ):
+            q = zi(n + 1)
+            cols = quad_cols(q)
+            back = nt(act, wd[q].reshape(QUAD, R))
             value = (
                 grad[rows, cols].astype(F32) + inv * (back * gain[:, cols]) - base
                 - xin[rows, cols].astype(F32) * tilt
@@ -354,143 +392,61 @@
 
             @pl.when(sec > 0)
             def _():
-                hop(i, ch, res).start()
-
+                hop(i, n, res).start()
+
+        for n in range(NZ - 1):
+            spread_act(i, n, z).start()
         keep(i).start()
         return carry
 
     lax.fori_loop(0, NBLK, chain, 0)
 
-    def terms(q):
-        cols = quad_cols(q)
-        pd[q] = (tn(norm[:ROWS, cols], acts[...]) * (1.0 / TOK)).astype(BF16).reshape(2, 2, SHARD, R)
-        pu[q] = (tn(grad[:, cols], hidden[...]) * (1.0 / TOK)).astype(BF16).reshape(2, 2, SHARD, R)
-
-    def make(step):
-        q = zi(step)
-        terms(q)
-        put(f"Pu{step}", pu.at[q, :, ocore], qu.at[q], twin)
-        put(f"Pd{step}", pd.at[q, :, ocore], qd.at[q], twin)
-
-    def heard(step):
-        q = zi(step)
-        got(f"Pu{step}", qu.at[q], twin)
-        got(f"Pd{step}", qd.at[q], twin)
-
-    def cross(step):
-        q = zi(step)
-        xsend[q] = (pd[q, oxl, core].astype(F32) + qd[q, oxl].astype(F32)).astype(BF16)
-        put(f"X{step}", xsend.at[q], xrecv.at[q], side)
-
-    def send_up_half(j):
-        dist = 4 - j
-        for way, ahead, behind in ways:
-            d = 0 if way == "+" else 1
-            q = zi(dist if way == "+" else -dist)
-            order = ("p", "s") if way == "+" else ("s", "p")
-            for which in order:
-                lead = (way == "+") == (which == "s")
-                if j == 0 and not lead:
-                    continue
-                e, k = (xl, 0) if which == "s" else (oxl, 1)
-                value = pu[q, e, core].astype(F32) + qu[q, e].astype(F32)
-                if j >= 2 or (j == 1 and lead):
-                    got(f"RU{way}{j - 1}{which}", ru.at[d, j - 1, k], behind)
-                    value = value + ru[d, j - 1, k].astype(F32)
-                su[d, j, k] = value.astype(BF16)
-                put(f"RU{way}{j}{which}", su.at[d, j, k], ru.at[d, j, k], ahead)
-
-    def send_down_half(j):
-        dist = 4 - j
-        if j == 0:
-            got("X4", xrecv.at[zi(4)], side)
-        else:
-            for way, _, _ in ways:
-                step = dist if way == "+" else -dist
-                got(f"X{step}", xrecv.at[zi(step)], side)
-        for way, ahead, behind in ways:
-            d = 0 if way == "+" else 1
-            q = zi(dist if way == "+" else -dist)
-            part = pl.ds(0 if way == "+" else HALF, HALF)
-            if j == 0:
-                value = (
-                    pd[q, xl, core, part].astype(F32) + qd[q, xl, part].astype(F32)
-                    + xrecv[q, part].astype(F32)
-                )
-                sd[d, 0, part] = value.astype(BF16)
-                put(f"RD{way}0", sd.at[d, 0, part], rd.at[d, 0, part], ahead)
-                continue
-            value = (
-                pd[q, xl, core].astype(F32) + qd[q, xl].astype(F32) + xrecv[q].astype(F32)
-            )
-            sd[d, j] = value.astype(BF16)
-            if j == 1:
-                got(f"RD{way}0", rd.at[d, 0, part], behind)
-                sd[d, j, part] = (
-                    pd[q, xl, core, part].astype(F32) + qd[q, xl, part].astype(F32)
-                    + xrecv[q, part].astype(F32) + rd[d, 0, part].astype(F32)
-                ).astype(BF16)
+    own_n.wait()
+    for step in range(1, NZ):
+        got(f"N{step}", gather_n.at[zi(-step)], at_z(-step))
+        got(f"H{step}", gather_h.at[zi(-step)], at_z(-step))
+
+    def arrived(i):
+        for n in range(NZ - 1):
+            spread_grad(i, n, zi(-(n + 1))).wait_recv()
+            spread_act(i, n, zi(-(n + 1))).wait_recv()
+        own_grad(i).wait()
+
+    def add_terms(first, count, fresh):
+        rows = pl.ds(first, count * BLK)
+        depth = NZ * count * BLK
+        for h, (wide_ref, thin_ref) in enumerate(((gather_n, gather_a), (gather_g, gather_h))):
+            term = tn(
+                wide_ref[:, rows, :].reshape(depth, QUAD), thin_ref[:, rows, :].reshape(depth, R)
+            ).reshape(2, 2, SHARD, R)
+            if fresh:
+                total[h] = term
             else:
-                got(f"RD{way}{j - 1}", rd.at[d, j - 1], behind)
-                sd[d, j] = (value + rd[d, j - 1].astype(F32)).astype(BF16)
-            put(f"RD{way}{j}", sd.at[d, j], rd.at[d, j], ahead)
-
-    make(4)
-    make(3)
-    make(-3)
-    heard(4)
-    send_up_half(0)
-    cross(4)
-    make(2)
-    make(-2)
-    heard(3)
-    heard(-3)
-    send_up_half(1)
-    cross(3)
-    cross(-3)
-    make(1)
-    make(-1)
-    send_down_half(0)
-    make(0)
-    heard(2)
-    heard(-2)
-    send_up_half(2)
-    cross(2)
-    cross(-2)
-    heard(1)
-    heard(-1)
-    cross(1)
-    cross(-1)
-    heard(0)
-    cross(0)
-    send_down_half(1)
-    send_up_half(3)
-    send_down_half(2)
-    for way, _, behind in ways:
-        d = 0 if way == "+" else 1
-        got(f"RU{way}3p", ru.at[d, 3, 1], behind)
-    usend[...] = (
-        pu[z, oxl, core].astype(F32) + qu[z, oxl].astype(F32)
-        + ru[0, 3, 1].astype(F32) + ru[1, 3, 1].astype(F32)
-    ).astype(BF16)
-    put("UF", usend, urecv, side)
-    send_down_half(3)
-    for way, _, behind in ways:
-        d = 0 if way == "+" else 1
-        got(f"RU{way}3s", ru.at[d, 3, 0], behind)
-    got("UF", urecv, side)
-    final[:, pl.ds(R, R)] = (
-        pu[z, xl, core].astype(F32) + qu[z, xl].astype(F32)
-        + ru[0, 3, 0].astype(F32) + ru[1, 3, 0].astype(F32) + urecv[...].astype(F32)
-    )
-    got("X0", xrecv.at[z], side)
-    for way, _, behind in ways:
-        d = 0 if way == "+" else 1
-        got(f"RD{way}3", rd.at[d, 3], behind)
-    final[:, pl.ds(0, R)] = (
-        pd[z, xl, core].astype(F32) + qd[z, xl].astype(F32) + xrecv[z].astype(F32)
-        + rd[0, 3].astype(F32) + rd[1, 3].astype(F32)
-    )
+                total[h] += term
+
+    first = 0
+    for count in (2, 2, 2, 1, 1):
+        for i in range(first, first + count):
+            arrived(i)
+        add_terms(first * BLK, count, first == 0)
+        first += count
+
+    scale = 1.0 / TOK
+    for e in (oxl, xl):
+        for h in range(2):
+            tsend[h, e] = (total[h, e, ocore] * scale).astype(BF16)
+            name = f"T{h}" + ("p" if e is oxl else "s")
+            put(name, tsend.at[h, e], trecv.at[h, e], twin)
+    for h in range(2):
+        got(f"T{h}p", trecv.at[h, oxl], twin)
+        xsend[h] = (total[h, oxl, core] * scale + trecv[h, oxl].astype(F32)).astype(BF16)
+        put(f"X{h}", xsend.at[h], xrecv.at[h], side)
+    for h in range(2):
+        got(f"T{h}s", trecv.at[h, xl], twin)
+        total[h, xl, core] = total[h, xl, core] * scale + trecv[h, xl].astype(F32)
+    for h in range(2):
+        got(f"X{h}", xrecv.at[h], side)
+        final[:, pl.ds(h * R, R)] = total[h, xl, core] + xrecv[h].astype(F32)
     store = pltpu.make_async_copy(final, ag_h.at[0], lsem.at[6])
     store.start()
 
@@ -500,9 +456,12 @@
     def settle(i, carry):
         @pl.when(sec > 0)
         def _():
-            for ch in range(NCH):
-                hop(i, ch, res).wait_send()
-
+            for n in range(NZ):
+                hop(i, n, res).wait_send()
+
+        for n in range(NZ - 1):
+            spread_grad(i, n, z).wait_send()
+            spread_act(i, n, z).wait_send()
         keep(i).wait()
         return carry
 
@@ -541,23 +500,24 @@
             pltpu.VMEM((ROWS, 1), F32),
             pltpu.VMEM((ROWS, 1), F32),
             pltpu.VMEM((ROWS, 1), F32),
-            pltpu.VMEM((NZ, 2, 2, SHARD, R), BF16),
-            pltpu.VMEM((NZ, 2, 2, SHARD, R), BF16),
-            pltpu.VMEM((NZ, 2, SHARD, R), BF16),
-            pltpu.VMEM((NZ, 2, SHARD, R), BF16),
-            pltpu.VMEM((NZ, SHARD, R), BF16),
-            pltpu.VMEM((NZ, SHARD, R), BF16),
-            pltpu.VMEM((2, 4, 2, SHARD, R), BF16),
-            pltpu.VMEM((2, 4, 2, SHARD, R), BF16),
-            pltpu.VMEM((2, 4, SHARD, R), BF16),
-            pltpu.VMEM((2, 4, SHARD, R), BF16),
-            pltpu.VMEM((SHARD, R), BF16),
-            pltpu.VMEM((SHARD, R), BF16),
+            pltpu.VMEM((NZ, ROWS, QUAD), BF16),
+            pltpu.VMEM((NZ, ROWS, QUAD), BF16),
+            pltpu.VMEM((NZ, ROWS, R), BF16),
+            pltpu.VMEM((NZ, ROWS, R), BF16),
+            pltpu.VMEM((2, 2, 2, SHARD, R), F32),
+            pltpu.VMEM((2, 2, SHARD, R), BF16),
+            pltpu.VMEM((2, 2, SHARD, R), BF16),
+            pltpu.VMEM((2, SHARD, R), BF16),
+            pltpu.VMEM((2, SHARD, R), BF16),
             pltpu.VMEM((SHARD, 2 * R), F32),
             pltpu.SemaphoreType.DMA((NSEM,)),
             pltpu.SemaphoreType.DMA((NSEM,)),
-            pltpu.SemaphoreType.DMA((NBLK * NCH,)),
-            pltpu.SemaphoreType.DMA((NBLK * NCH,)),
+            pltpu.SemaphoreType.DMA((NBLK * NZ,)),
+            pltpu.SemaphoreType.DMA((NBLK * NZ,)),
+            pltpu.SemaphoreType.DMA((NBLK * NZ,)),
+            pltpu.SemaphoreType.DMA((NBLK * NZ,)),
+            pltpu.SemaphoreType.DMA((NBLK * NZ,)),
+            pltpu.SemaphoreType.DMA((NBLK * NZ,)),
             pltpu.SemaphoreType.DMA((NBLK,)),
             pltpu.SemaphoreType.DMA((8,)),
         ],

time: 212 us -> 196 us (0.925)
  Pallas kernels: 207 us -> 191 us
    pallas_call x1, Pallas kernels: 207 us -> 191 us  [per_device(): pl.pallas_call(kernel, out_shape=(jax.ShapeDtypeStruct((1, 2, TOK, D), BF...]
where the time goes in v2:
time: 196 us
  Pallas kernels  191 us (97%)
  local copies, waits for them, and re-layouts  4.1 us (2%)
    pallas_call x1, Pallas kernels, per_device(): pl.pallas_call(kernel, out_shape=(jax.ShapeDtypeStruct((1, 2, TOK, D), BF...  191 us
    unnamed x4, local copies, waits for them, and re-layouts  4.1 us

profile of v2, /device:TPU:1, one launch (start us, length us, event | category | flops | bytes accessed | tf_op | source)
XLA Modules:
  0.0 195.7 jit_solution(14847084751302597530)
XLA Ops:
  0.6 190.9 %shard_map.104 = (bf16[1,2,64,9216]{3,2,1,0:T(8,128)(2,1)}, f32[1,288,512]{2,1,0:T(8,128)}) custom-call(bf16[1,2,64,9216]{3,2,1,0:T(8,128)(2,1)} %hist_h.1, s32[1,2,64,9216]{3,2,1,0:T(8,128)} %codes_h.1, f32[1,2,64]{2,1,0:T(2,128)} %scales.1, s32[1,2]{1,0:T(1,128)} %ids.1, bf16[2,64,9216]{2,1,0:T(8,128)(2,1)} %cot_h.1, f32[1,9216]{1,0:T(1,128)} %gain.1, ...), custom_call_target="tpu_custom_call" | custom-call | flops 3019898880 | bytes 25165824 | tf_op jit(solution)/shard_map/pallas_call | solution.py:477
  191.6 0.0 copy-start
  191.6 3.3 %copy.13 = bf16[1,2,64,9216]{3,2,1,0:T(8,128)(2,1)} copy(bf16[1,2,64,9216]{3,2,1,0:T(8,128)(2,1)} %get-tuple-element.4) | data formatting | bytes 4718592
  194.8 0.0 copy-done
  194.8 0.8 copy.14
Async XLA Ops:
  191.6 3.3 %copy-start = (f32[1,288,512]{2,1,0:T(8,128)S(1)}, f32[1,288,512]{2,1,0:T(8,128)}, u32[]{:S(2)}) copy-start(f32[1,288,512]{2,1,0:T(8,128)} %get-tuple-element.5) | copy-start | bytes 1769476

commit v3 on v2

--- a/solution.py
+++ b/solution.py
@@ -23,7 +23,7 @@
 NBLK = ROWS // BLK
 ECH = 8
 ECW = D // ECH
-NSEM = 96
+NSEM = 128
 F32 = jnp.float32
 BF16 = jnp.bfloat16
 
@@ -304,16 +304,59 @@
         for m in range(2):
             seed(m).wait()
 
-    for step in range(1, NZ):
-        q = zi(step)
-        put(f"N{step}", norm.at[pl.ds(0, ROWS), quad_cols(q)], gather_n.at[z], at_z(step))
     own_n = pltpu.make_async_copy(
         norm.at[pl.ds(0, ROWS), quad_cols(z)], gather_n.at[z], lsem.at[7]
     )
     own_n.start()
-    for step in range(1, NZ):
-        put(f"H{step}", hidden, gather_h.at[z], at_z(step))
+
+    def spread_norm(step):
+        return link(
+            f"N{step}", norm.at[pl.ds(0, ROWS), quad_cols(zi(step))], gather_n.at[z], at_z(step)
+        )
+
+    def tour_rows(first, count, dist, way):
+        if dist < 4:
+            return pl.ds(first, count)
+        half = count // (2 * BLK) * BLK
+        return pl.ds(first, half) if way == "+" else pl.ds(first + half, count - half)
+
+    def tour_links(name, src, dst, first, count, stage):
+        copies = []
+        for way, ahead, _ in ways:
+            q = zi(-stage if way == "+" else stage)
+            rows = tour_rows(first, count, stage + 1, way)
+            held = src.at[rows] if stage == 0 else dst.at[q, rows]
+            copies.append(link(f"{name}{way}{stage}", held, dst.at[q, rows], ahead))
+        return copies
+
+    def tour(name, src, dst, first, count, stage):
+        if stage > 0:
+            for way, _, behind in ways:
+                q = zi(-stage if way == "+" else stage)
+                rows = tour_rows(first, count, stage, way)
+                got(f"{name}{way}{stage - 1}", dst.at[q, rows], behind)
+        if stage < 4:
+            for copy in tour_links(name, src, dst, first, count, stage):
+                copy.start()
+
+    def tour_sent(name, src, dst, first, count):
+        for stage in range(4):
+            for copy in tour_links(name, src, dst, first, count, stage):
+                copy.wait_send()
+
     gather_h[z] = hidden[...]
+
+    @pl.when(sec <= 1)
+    def _():
+        for stage in range(5):
+            tour("Ha", hidden, gather_h, 0, ROWS, stage)
+            for step in ((4,), (3, 5), (2, 6), (1, 7), ())[stage]:
+                spread_norm(step).start()
+
+    @pl.when(sec > 1)
+    def _():
+        for step in range(1, NZ):
+            spread_norm(step).start()
 
     def rows_of(i):
         return pl.ds(pl.multiple_of(i * BLK, BLK), BLK)
@@ -374,6 +417,12 @@
         act = (lift * slopes[rows, :]).astype(BF16)
         acts[rows, :] = act
         gather_a[z, rows, :] = act
+
+        @pl.when(sec <= 1)
+        def _():
+            for n in range(NZ - 1):
+                spread_act(i, n, z).start()
+
         wide = act.astype(F32)
         m1 = jnp.sum(wide * ugain[...], axis=1, keepdims=True) * (1.0 / D)
         m2 = jnp.sum(wide * qmat[rows, :], axis=1, keepdims=True) * (1.0 / D)
@@ -394,64 +443,94 @@
             def _():
                 hop(i, n, res).start()
 
-        for n in range(NZ - 1):
-            spread_act(i, n, z).start()
         keep(i).start()
         return carry
 
     lax.fori_loop(0, NBLK, chain, 0)
+
+    @pl.when(sec > 1)
+    def _():
+        for stage in range(5):
+            tour("Ad", acts, gather_a, 0, ROWS, stage)
+            tour("Hb", hidden, gather_h, 0, ROWS, stage)
 
     own_n.wait()
     for step in range(1, NZ):
         got(f"N{step}", gather_n.at[zi(-step)], at_z(-step))
-        got(f"H{step}", gather_h.at[zi(-step)], at_z(-step))
-
-    def arrived(i):
+
+    def arrived(h, i):
         for n in range(NZ - 1):
-            spread_grad(i, n, zi(-(n + 1))).wait_recv()
-            spread_act(i, n, zi(-(n + 1))).wait_recv()
-        own_grad(i).wait()
-
-    def add_terms(first, count, fresh):
-        rows = pl.ds(first, count * BLK)
+            if h == 1:
+                spread_grad(i, n, zi(-(n + 1))).wait_recv()
+            else:
+                spread_act(i, n, zi(-(n + 1))).wait_recv()
+        if h == 1:
+            own_grad(i).wait()
+
+    def add_terms(h, first, count):
+        if h == 1:
+            for i in range(first, first + count):
+                arrived(1, i)
+        else:
+            @pl.when(sec <= 1)
+            def _():
+                for i in range(first, first + count):
+                    arrived(0, i)
+
+        rows = pl.ds(first * BLK, count * BLK)
         depth = NZ * count * BLK
-        for h, (wide_ref, thin_ref) in enumerate(((gather_n, gather_a), (gather_g, gather_h))):
-            term = tn(
-                wide_ref[:, rows, :].reshape(depth, QUAD), thin_ref[:, rows, :].reshape(depth, R)
-            ).reshape(2, 2, SHARD, R)
-            if fresh:
-                total[h] = term
-            else:
-                total[h] += term
-
-    first = 0
-    for count in (2, 2, 2, 1, 1):
-        for i in range(first, first + count):
-            arrived(i)
-        add_terms(first * BLK, count, first == 0)
-        first += count
+        wide_ref, thin_ref = ((gather_n, gather_a), (gather_g, gather_h))[h]
+        term = tn(
+            wide_ref[:, rows, :].reshape(depth, QUAD), thin_ref[:, rows, :].reshape(depth, R)
+        ).reshape(2, 2, SHARD, R)
+        if first == 0:
+            total[h] = term
+        else:
+            total[h] += term
+
+    def to_twin(h):
+        for e, which in ((oxl, "p"), (xl, "s")):
+            tsend[h, e] = (total[h, e, ocore] * scale).astype(BF16)
+            put(f"T{h}{which}", tsend.at[h, e], trecv.at[h, e], twin)
 
     scale = 1.0 / TOK
-    for e in (oxl, xl):
-        for h in range(2):
-            tsend[h, e] = (total[h, e, ocore] * scale).astype(BF16)
-            name = f"T{h}" + ("p" if e is oxl else "s")
-            put(name, tsend.at[h, e], trecv.at[h, e], twin)
-    for h in range(2):
+    for first, count in ((0, 3), (3, 3), (6, 1)):
+        for h in (1, 0):
+            add_terms(h, first, count)
+    add_terms(1, 7, 1)
+    to_twin(1)
+
+    def to_side(h):
         got(f"T{h}p", trecv.at[h, oxl], twin)
         xsend[h] = (total[h, oxl, core] * scale + trecv[h, oxl].astype(F32)).astype(BF16)
         put(f"X{h}", xsend.at[h], xrecv.at[h], side)
-    for h in range(2):
+
+    to_side(1)
+    add_terms(0, 7, 1)
+    to_twin(0)
+    to_side(0)
+    for h in (1, 0):
         got(f"T{h}s", trecv.at[h, xl], twin)
         total[h, xl, core] = total[h, xl, core] * scale + trecv[h, xl].astype(F32)
-    for h in range(2):
+    for h in (1, 0):
         got(f"X{h}", xrecv.at[h], side)
         final[:, pl.ds(h * R, R)] = total[h, xl, core] + xrecv[h].astype(F32)
     store = pltpu.make_async_copy(final, ag_h.at[0], lsem.at[6])
     store.start()
 
+    for step in range(1, NZ):
+        spread_norm(step).wait_send()
     for copy in pending:
         copy.wait_send()
+
+    @pl.when(sec <= 1)
+    def _():
+        tour_sent("Ha", hidden, gather_h, 0, ROWS)
+
+    @pl.when(sec > 1)
+    def _():
+        tour_sent("Ad", acts, gather_a, 0, ROWS)
+        tour_sent("Hb", hidden, gather_h, 0, ROWS)
 
     def settle(i, carry):
         @pl.when(sec > 0)
@@ -461,7 +540,12 @@
 
         for n in range(NZ - 1):
             spread_grad(i, n, z).wait_send()
-            spread_act(i, n, z).wait_send()
+
+        @pl.when(sec <= 1)
+        def _():
+            for n in range(NZ - 1):
+                spread_act(i, n, z).wait_send()
+
         keep(i).wait()
         return carry
 

time: 196 us -> 193 us (0.985)
  Pallas kernels: 191 us -> 189 us
    pallas_call x1, Pallas kernels: 191 us -> 189 us  [per_device(): pl.pallas_call(kernel, out_shape=(jax.ShapeDtypeStruct((1, 2, TOK, D), BF...]
where the time goes in v3:
time: 193 us
  Pallas kernels  189 us (98%)
  local copies, waits for them, and re-layouts  4.1 us (2%)
    pallas_call x1, Pallas kernels, per_device(): pl.pallas_call(kernel, out_shape=(jax.ShapeDtypeStruct((1, 2, TOK, D), BF...  189 us
    unnamed x4, local copies, waits for them, and re-layouts  4.1 us

profile of v3, /device:TPU:1, one launch (start us, length us, event | category | flops | bytes accessed | tf_op | source)
XLA Modules:
  0.0 193.3 jit_solution(8175047288357445013)
XLA Ops:
  0.6 188.5 %shard_map.104 = (bf16[1,2,64,9216]{3,2,1,0:T(8,128)(2,1)}, f32[1,288,512]{2,1,0:T(8,128)}) custom-call(bf16[1,2,64,9216]{3,2,1,0:T(8,128)(2,1)} %hist_h.1, s32[1,2,64,9216]{3,2,1,0:T(8,128)} %codes_h.1, f32[1,2,64]{2,1,0:T(2,128)} %scales.1, s32[1,2]{1,0:T(1,128)} %ids.1, bf16[2,64,9216]{2,1,0:T(8,128)(2,1)} %cot_h.1, f32[1,9216]{1,0:T(1,128)} %gain.1, ...), custom_call_target="tpu_custom_call" | custom-call | flops 3019898880 | bytes 25165824 | tf_op jit(solution)/shard_map/pallas_call | solution.py:561
  189.2 0.0 copy-start
  189.2 3.3 %copy.13 = bf16[1,2,64,9216]{3,2,1,0:T(8,128)(2,1)} copy(bf16[1,2,64,9216]{3,2,1,0:T(8,128)(2,1)} %get-tuple-element.4) | data formatting | bytes 4718592
  192.5 0.0 copy-done
  192.5 0.8 copy.14
Async XLA Ops:
  189.2 3.3 %copy-start = (f32[1,288,512]{2,1,0:T(8,128)S(1)}, f32[1,288,512]{2,1,0:T(8,128)}, u32[]{:S(2)}) copy-start(f32[1,288,512]{2,1,0:T(8,128)} %get-tuple-element.5) | copy-start | bytes 1769476

commit v4 on v3

--- a/solution.py
+++ b/solution.py
@@ -21,6 +21,7 @@
 HALF = SHARD // 2
 BLK = 16
 NBLK = ROWS // BLK
+STEPS = (4, 3, 5, 2, 6, 1, 7, 0)
 ECH = 8
 ECW = D // ECH
 NSEM = 128
@@ -362,7 +363,7 @@
         return pl.ds(pl.multiple_of(i * BLK, BLK), BLK)
 
     def hop(i, n, src):
-        part = (rows_of(i), quad_cols(zi(n + 1)))
+        part = (rows_of(i), quad_cols(zi(STEPS[n])))
         index = i * NZ + n
         return pltpu.make_async_remote_copy(
             src_ref=src.at[part], dst_ref=grad.at[part],
@@ -373,10 +374,10 @@
     def spread_grad(i, n, landing):
         index = i * NZ + n
         return pltpu.make_async_remote_copy(
-            src_ref=grad.at[rows_of(i), quad_cols(zi(n + 1))],
+            src_ref=grad.at[rows_of(i), quad_cols(zi(STEPS[n]))],
             dst_ref=gather_g.at[landing, rows_of(i)],
             send_sem=gss.at[index], recv_sem=grs.at[index],
-            device_id=at_z(n + 1), device_id_type=MESH,
+            device_id=at_z(STEPS[n]), device_id_type=MESH,
         )
 
     def own_grad(i):
@@ -390,7 +391,7 @@
         return pltpu.make_async_remote_copy(
             src_ref=acts.at[rows_of(i)], dst_ref=gather_a.at[landing, rows_of(i)],
             send_sem=ass.at[index], recv_sem=ars.at[index],
-            device_id=at_z(n + 1), device_id_type=MESH,
+            device_id=at_z(STEPS[n]), device_id_type=MESH,
         )
 
     def keep(i):
@@ -403,7 +404,7 @@
         rows = rows_of(i)
         lift = jnp.zeros((BLK, R), F32)
         for n in range(NZ):
-            q = zi(n + 1)
+            q = zi(STEPS[n])
 
             @pl.when(sec < NSEC - 1)
             def _():
@@ -430,7 +431,7 @@
         tilt = inv * inv * m2
         base = inv * m1 - mean * tilt
         for n in range(NZ):
-            q = zi(n + 1)
+            q = zi(STEPS[n])
             cols = quad_cols(q)
             back = nt(act, wd[q].reshape(QUAD, R))
             value = (
@@ -461,9 +462,9 @@
     def arrived(h, i):
         for n in range(NZ - 1):
             if h == 1:
-                spread_grad(i, n, zi(-(n + 1))).wait_recv()
+                spread_grad(i, n, zi(-STEPS[n])).wait_recv()
             else:
-                spread_act(i, n, zi(-(n + 1))).wait_recv()
+                spread_act(i, n, zi(-STEPS[n])).wait_recv()
         if h == 1:
             own_grad(i).wait()
 

time: 193 us -> 192 us (level)
  Pallas kernels: 189 us -> 187 us
where the time goes in v4:
time: 192 us
  Pallas kernels  187 us (97%)
  local copies, waits for them, and re-layouts  4.1 us (2%)
    pallas_call x1, Pallas kernels, per_device(): pl.pallas_call(kernel, out_shape=(jax.ShapeDtypeStruct((1, 2, TOK, D), BF...  187 us
    unnamed x4, local copies, waits for them, and re-layouts  4.1 us

profile of v4, /device:TPU:1, one launch (start us, length us, event | category | flops | bytes accessed | tf_op | source)
XLA Modules:
  0.0 191.7 jit_solution(18320336912836556368)
XLA Ops:
  0.6 187.0 %shard_map.104 = (bf16[1,2,64,9216]{3,2,1,0:T(8,128)(2,1)}, f32[1,288,512]{2,1,0:T(8,128)}) custom-call(bf16[1,2,64,9216]{3,2,1,0:T(8,128)(2,1)} %hist_h.1, s32[1,2,64,9216]{3,2,1,0:T(8,128)} %codes_h.1, f32[1,2,64]{2,1,0:T(2,128)} %scales.1, s32[1,2]{1,0:T(1,128)} %ids.1, bf16[2,64,9216]{2,1,0:T(8,128)(2,1)} %cot_h.1, f32[1,9216]{1,0:T(1,128)} %gain.1, ...), custom_call_target="tpu_custom_call" | custom-call | flops 3019898880 | bytes 25165824 | tf_op jit(solution)/shard_map/pallas_call | solution.py:562
  187.6 0.0 copy-start
  187.6 3.3 %copy.13 = bf16[1,2,64,9216]{3,2,1,0:T(8,128)(2,1)} copy(bf16[1,2,64,9216]{3,2,1,0:T(8,128)(2,1)} %get-tuple-element.4) | data formatting | bytes 4718592
  190.9 0.0 copy-done
  190.9 0.8 copy.14
Async XLA Ops:
  187.6 3.3 %copy-start = (f32[1,288,512]{2,1,0:T(8,128)S(1)}, f32[1,288,512]{2,1,0:T(8,128)}, u32[]{:S(2)}) copy-start(f32[1,288,512]{2,1,0:T(8,128)} %get-tuple-element.5) | copy-start | bytes 1769476
